TPU v7x, 32 devices: a whole 2x2x4 slice. The times are simulated.
32 devices in a mesh: ctx: 2 (over x), head: 4 (over y, core), rep: 4 (over z).
Axes of the slice: x: 2, y: 2, z: 4, core: 2. Of those that a mesh axis runs over, the one named last changes fastest.
Arguments:
- kv_cache: float32 [8, 2, 512, 8, 128], P('head', None, 'ctx', 'rep'), may hold values from -8 to 8
- prefill_q: float32 [8, 256, 64, 128], P('head', 'ctx', 'rep'), may hold values from -512 to 512
- decode_q: float32 [8, 8, 4, 64, 128], P(None, ('ctx', 'rep'), None, 'head'), may hold values from -512 to 512
- decode_kv: float32 [8, 8, 4, 2, 8, 128], P(None, ('ctx', 'rep'), None, None, 'head'), may hold values from -12 to 12
- lengths: int32 [8], replicated, may hold values from 256 to 512, as said below
- row_length: int32 [8, 8], P(None, ('ctx', 'rep')), may hold values from 2 to 512, as said below
Outputs:
- prefill_out: float32 [8, 256, 64, 128], P('head', 'ctx', 'rep')
- decode_out: float32 [8, 8, 4, 64, 128], P(None, ('ctx', 'rep'), None, 'head')
Inputs may be any that keep to these rules, and one draw needn't show every extreme that they name: `lengths`: multiples of 128; some request has length 512. `row_length`: a row reads at most its request's length; every request has a row that reads its whole length.
All inputs are finite; a program needn't handle non-finite values.
Results may differ from a plain program's by a relative error of at most 0.0003.
Values sent between devices are 32-bit elements; how exact they have to be, the bound alone decides.
No kernel may reach another device: no remote copies, remote signals or barrier semaphores. Data moves between devices by JAX's collectives and lax.ppermute only.
A program may use at most 128 MiB of HBM per device.

v0:
```python
import math
import jax
import jax.numpy as jnp
from jax import lax
from jax.sharding import PartitionSpec as P

NEG_FILL = -1e30
HIGH_PRECISION = lax.Precision.HIGHEST


def broadcast(value, axis, source):
    kept = jnp.where(lax.axis_index(axis) == source, value, 0).astype(value.dtype)
    return lax.psum(kept, axis)


def online_fold(running, scores, value_rows, pattern):
    run_max, run_total, run_acc = running
    new_max = jnp.maximum(run_max, jnp.max(scores, axis=-1))
    weights = jnp.exp(scores - new_max[..., None])
    new_total = jnp.sum(weights, axis=-1)
    new_acc = jnp.einsum(pattern, weights, value_rows, precision=HIGH_PRECISION)
    return (new_max, new_total, new_acc)


def empty_state(lead_shape, head_dim):
    return (
        jnp.full(lead_shape, NEG_FILL, jnp.float32),
        jnp.zeros(lead_shape, jnp.float32),
        jnp.zeros(lead_shape + (head_dim,), jnp.float32),
    )


def block_fold(running, query_rows, key_block, first_pos, limits, score_scale, strict):
    block_len = key_block.shape[2]
    scores = (
        jnp.einsum("bkrd,bnkd->bkrn", query_rows, key_block[:, 0], precision=HIGH_PRECISION)
        * score_scale
    )
    positions = first_pos + jnp.arange(block_len, dtype=jnp.int32)
    if strict:
        allowed = positions[None, None, :] < limits[:, :, None]
    else:
        allowed = positions[None, None, :] <= limits[:, :, None]
    scores = jnp.where(allowed[:, None], scores, NEG_FILL)
    return online_fold(running, scores, key_block[:, 1], "bkrn,bnkd->bkrd")


def source_major(values, slot_count, kv_heads, sources, count_rows, step_count, group_size):
    tail_shape = values.shape[3:]
    spread_out = values.reshape(
        (slot_count, kv_heads, sources, count_rows, step_count, group_size) + tail_shape
    )
    axes_order = (2, 0, 3, 4, 1, 5) + tuple(range(6, 6 + len(tail_shape)))
    moved = jnp.transpose(spread_out, axes_order)
    return moved.reshape(
        (sources, slot_count, count_rows, step_count, kv_heads * group_size) + tail_shape
    )


def on_device(kv_cache, prefill_q, decode_q, decode_kv, lengths, row_length):
    ctx_count = lax.axis_size("ctx")
    ctx_index = lax.axis_index("ctx")
    head_index = lax.axis_index("head")
    req_group, span_rows, rep_heads, head_dim = prefill_q.shape
    rep_kv = kv_cache.shape[3]
    group_size = rep_heads // rep_kv
    block_len = kv_cache.shape[2]
    score_scale = 1.0 / math.sqrt(head_dim)
    group_lengths = lax.dynamic_slice_in_dim(lengths, head_index * req_group, req_group)
    span_pos = (
        group_lengths[:, None]
        - span_rows * ctx_count
        + ctx_index * span_rows
        + jnp.arange(span_rows, dtype=jnp.int32)[None, :]
    )
    row_pos = jnp.repeat(span_pos, group_size, axis=1)
    prefill_rows = jnp.transpose(
        prefill_q.reshape(req_group, span_rows, rep_kv, group_size, head_dim), (0, 2, 1, 3, 4)
    ).reshape(req_group, rep_kv, span_rows * group_size, head_dim)
    start_state = empty_state((req_group, rep_kv, span_rows * group_size), head_dim)
    run_max, run_total, run_acc = block_fold(
        start_state,
        prefill_rows,
        lax.all_gather(kv_cache, "ctx", axis=2, tiled=True),
        jnp.int32(0),
        row_pos,
        score_scale,
        False,
    )
    prefill_vals = run_acc / run_total[..., None]
    prefill_out = jnp.transpose(
        prefill_vals.reshape(req_group, rep_kv, span_rows, group_size, head_dim), (0, 2, 1, 3, 4)
    ).reshape(prefill_q.shape)
    all_requests = lax.all_gather(kv_cache, "head", axis=0, tiled=True)
    head_cache = broadcast(all_requests, "rep", head_index)
    requests, row_count, step_count, local_heads, unused_dim = decode_q.shape
    kv_heads = local_heads // group_size
    gathered_rows, gathered_limits = (
        lax.all_gather(decode_q, "ctx", axis=1, tiled=True),
        lax.all_gather(row_length, "ctx", axis=1, tiled=True),
    )
    total_rows = gathered_rows.shape[1]
    grouped = jnp.transpose(
        gathered_rows.reshape(requests, total_rows, step_count, kv_heads, group_size, head_dim),
        (0, 3, 1, 2, 4, 5),
    ).reshape(requests, kv_heads, -1, head_dim)
    limits = jnp.broadcast_to(
        gathered_limits[:, :, None, None], (requests, total_rows, step_count, group_size)
    ).reshape(requests, -1)
    running = empty_state((requests, kv_heads, grouped.shape[2]), head_dim)
    running = block_fold(
        running, grouped, head_cache, ctx_index * block_len, limits, score_scale, True
    )
    shaped = tuple(
        (
            source_major(values, requests, kv_heads, ctx_count, row_count, step_count, group_size)
            for values in running
        )
    )
    home_max, home_total, home_acc = (
        lax.all_to_all(shaped[0], "ctx", split_axis=0, concat_axis=0, tiled=True),
        lax.all_to_all(shaped[1], "ctx", split_axis=0, concat_axis=0, tiled=True),
        lax.all_to_all(shaped[2], "ctx", split_axis=0, concat_axis=0, tiled=True),
    )
    ctx_max = jnp.max(home_max, axis=0)
    factor = jnp.exp(home_max - ctx_max[None])
    ctx_total = jnp.sum(home_total * factor, axis=0)
    ctx_acc = jnp.sum(home_acc * factor[..., None], axis=0)
    home_rows = decode_q.reshape(requests, row_count, step_count, kv_heads, group_size, head_dim)
    draft_scores = (
        jnp.einsum(
            "artkgd,arskd->artkgs", home_rows, decode_kv[:, :, :, 0], precision=HIGH_PRECISION
        )
        * score_scale
    )
    step_ids = jnp.arange(step_count, dtype=jnp.int32)
    causal = step_ids[None, :] <= step_ids[:, None]
    draft_scores = jnp.where(causal[None, None, :, None, None, :], draft_scores, NEG_FILL)
    ctx_max = ctx_max.reshape(requests, row_count, step_count, kv_heads, group_size)
    ctx_total = ctx_total.reshape(requests, row_count, step_count, kv_heads, group_size)
    ctx_acc = ctx_acc.reshape(requests, row_count, step_count, kv_heads, group_size, head_dim)
    joint_max = jnp.maximum(ctx_max, jnp.max(draft_scores, axis=-1))
    draft_weights = jnp.exp(draft_scores - joint_max[..., None])
    ctx_factor = jnp.exp(ctx_max - joint_max)
    denominator = ctx_total * ctx_factor + jnp.sum(draft_weights, axis=-1)
    numerator = ctx_acc * ctx_factor[..., None] + jnp.einsum(
        "artkgs,arskd->artkgd", draft_weights, decode_kv[:, :, :, 1], precision=HIGH_PRECISION
    )
    decode_out = (numerator / denominator[..., None]).reshape(decode_q.shape)
    return (prefill_out, decode_out)


def solution(mesh):
    in_specs = (
        P("head", None, "ctx", "rep", None),
        P("head", "ctx", "rep", None),
        P(None, ("ctx", "rep"), None, "head", None),
        P(None, ("ctx", "rep"), None, None, "head", None),
        P(),
        P(None, ("ctx", "rep")),
    )
    out_specs = (P("head", "ctx", "rep", None), P(None, ("ctx", "rep"), None, "head", None))
    return jax.shard_map(
        on_device, mesh=mesh, in_specs=in_specs, out_specs=out_specs, check_vma=False
    )
```

profile of v0, /device:TPU:0, one launch (start us, length us, event | category | flops | bytes accessed | tf_op | source)
XLA Modules:
  0.0 285.3 jit_solution(5755422686790085839)
XLA Ops:
  7.2 0.0 copy-start
  7.2 0.0 all-gather.6.cloned.1.call-start
  7.2 2.4 copy.82
  9.6 0.0 all-gather.6.cloned.1.call-update
  9.7 0.0 all-gather.4.cloned.1.call-start
  9.7 0.7 all-gather.4.cloned.1.call-update
  10.4 0.0 all-reduce.2.cloned.1.call-start
  10.5 36.9 %all-gather.6.cloned.1.call-done = f32[8,2,256,2,128]{4,2,3,0,1:T(8,128)} async-done(((f32[2,2,256,2,128]{4,2,3,0,1:T(8,128)}), f32[8,2,256,2,128]{4,2,3,0,1:T(8,128)}) %all-gather.6.cloned.1.call-update) | async-done | bytes 4194320 | tf_op jit(solution)/shard_map/all_gather | solution.py:94
  47.4 4.6 %broadcast_select_fusion = f32[8,2,256,2,128]{4,2,3,0,1:T(8,128)} fusion(f32[8,2,256,2,128]{4,2,3,0,1:T(8,128)} %all-gather.6.cloned.1.call-done, pred[]{:T(512)S(6)} %eq.3), kind=kLoop, calls=%fused_computation.18 | loop fusion | flops 1048576 | bytes 8388609 | tf_op jit(solution)/shard_map/jit(_where)/select_n | solution.py:12
  52.0 0.0 all-reduce.2.cloned.1.call-update
  52.0 0.6 copy-done.5
  52.6 4.2 %all-gather = s32[2,1,8]{2,1,0:T(1,128)S(1)} all-gather(s32[1,1,8]{2,1,0:T(1,128)S(1)} %bitcast.147), channel_id=1, replica_groups=mesh['ctx'=2,'head'=4,'rep'=4] {'ctx'}, dimensions={0}, use_global_device_ids=true | all-gather | bytes 96 | tf_op jit(solution)/shard_map/all_gather | solution.py:100
  56.8 0.1 copy.85
  56.9 0.1 broadcast_in_dim.76
  57.0 0.1 lt.24
  57.1 0.0 copy-done.4
  57.1 0.1 add_add_fusion
  57.2 0.1 iota_add_fusion.1
  57.2 0.1 broadcast_in_dim.48
  57.3 0.1 le.37
  57.5 0.0 copy-done.1
  57.5 12.6 %all_gather.15 = f32[8,2,4,16,128]{4,3,2,1,0:T(8,128)S(1)} all-gather(f32[8,1,4,16,128]{4,3,2,1,0:T(8,128)S(1)} %copy-done.1), channel_id=1, replica_groups=mesh['ctx'=2,'head'=4,'rep'=4] {'ctx'}, dimensions={1}, use_global_device_ids=true | all-gather | bytes 786432 | tf_op jit(solution)/shard_map/all_gather | solution.py:99
  70.0 0.9 copy.87
  70.9 0.0 copy-done.3
  71.0 0.1 broadcast_compare_fusion
  71.1 3.6 %fusion.31 = (f32[8,4,2,8]{3,1,2,0:T(4,128)S(1)}, f32[8,1,4,2,8,4]{4,5,2,3,0,1:T(4,128)S(1)}) fusion(f32[8,1,4,1,2,128]{5,4,3,2,1,0:T(2,128)S(1)} %get-tuple-element.13, pred[4,4]{1,0:T(4,128)(4,1)S(1)} %iota_compare_fusion.1, f32[8,1,4,16,128]{4,3,2,1,0:T(8,128)S(1)} %copy-done.1), kind=kOutput, calls=%fused_computation.63 | convolution fusion | flops 3151360 | bytes 305168 | tf_op jit(solution)/shard_map/artkgd,arskd->artkgs/dot_general | solution.py:131
  74.7 0.6 iota_compare_fusion
  75.3 10.6 %all-gather.4.cloned.1.call-done = f32[2,2,512,2,128]{4,2,3,0,1:T(8,128)} async-done(((f32[2,2,256,2,128]{4,2,3,0,1:T(8,128)}), f32[2,2,512,2,128]{4,2,3,0,1:T(8,128)}) %all-gather.4.cloned.1.call-update) | async-done | bytes 2097168 | tf_op jit(solution)/shard_map/all_gather | solution.py:84
  86.0 0.0 copy-done
  86.0 9.6 %fusion = (f32[2,2,1024]{2,1,0:T(2,128)S(1)}, f32[2,2,1024,512]{2,3,1,0:T(8,128)S(1)}) fusion(pred[2,1024,512]{1,2,0:T(8,128)(4,1)S(1)} %iota_compare_fusion, f32[2,2,512,2,128]{4,2,3,0,1:T(8,128)} %all-gather.4.cloned.1.call-done, f32[2,128,16,128]{3,2,1,0:T(8,128)S(1)} %copy-done), kind=kOutput, calls=%fused_computation.2 | convolution fusion | flops 3227512832 | bytes 12599296 | tf_op jit(solution)/shard_map/bkrd,bnkd->bkrn/dot_general | solution.py:36
  95.6 0.0 copy-start.2
  95.6 2.2 fusion.1
  97.8 15.4 %divide_bitcast_fusion = f32[2,128,2,8,128]{4,3,1,2,0:T(8,128)S(1)} fusion(f32[2,2,1024]{2,1,0:T(2,128)S(1)} %fusion.1, f32[2,2,512,2,128]{4,2,3,0,1:T(8,128)S(1)} %copy-done.2, f32[2,2,1024,512]{2,3,1,0:T(8,128)S(1)} %get-tuple-element.17, f32[2,2,1024]{2,1,0:T(2,128)S(1)} %broadcast_maximum_fusion, pred[2,1024,512]{1,2,0:T(8,128)(4,1)S(1)} %iota_compare_fusion), kind=kOutput, calls=%fused_computation.19 | convolution fusion | flops 3228041216 | bytes 12615680 | tf_op jit(solution)/shard_map/bkrn,bnkd->bkrd/dot_general | solution.py:21
  113.3 1.5 copy.141
  114.8 130.5 %all-reduce.2.cloned.1.call-done = f32[8,2,256,2,128]{4,2,3,0,1:T(8,128)} async-done(((f32[8,2,256,2,128]{4,2,3,0,1:T(8,128)}), f32[8,2,256,2,128]{4,2,3,0,1:T(8,128)}) %all-reduce.2.cloned.1.call-update) | async-done | bytes 4194320 | tf_op jit(solution)/shard_map/psum | solution.py:13
  245.2 4.1 %fusion.30 = (f32[8,2,64]{2,1,0:T(2,128)S(1)}, f32[8,2,64,256]{3,2,1,0:T(8,128)S(1)}) fusion(f32[8,2,64,128]{3,2,1,0:T(8,128)} %bitcast.142, f32[8,2,256,2,128]{4,2,3,0,1:T(8,128)} %all-reduce.2.cloned.1.call-done, pred[8,64,256]{2,1,0:T(8,128)(4,1)S(1)} %broadcast_compare_fusion), kind=kOutput, calls=%fused_computation.62 | convolution fusion | flops 403438592 | bytes 3805184 | tf_op jit(solution)/shard_map/bkrd,bnkd->bkrn/dot_general | solution.py:36
  249.4 0.4 fusion.19
  249.8 0.1 reshape.223
  249.9 0.1 copy.101
  250.0 0.1 reshape.224
  250.1 0.7 reshape.235
  250.8 3.2 %all-to-all-start.2 = ((f32[2,1,512]{2,1,0:T(1,128)}), f32[2,1,512]{2,1,0:T(1,128)S(1)}, u32[]{:S(2)}, u32[]{:S(2)}) async-start(f32[2,1,512]{2,1,0:T(1,128)} %reshape.235), calls=%async_computation.2 | async-start | bytes 8192 | tf_op jit(solution)/shard_map/all_to_all | solution.py:122
  254.0 0.1 max_broadcast_in_dim.26
  254.1 0.1 copy.91
  254.2 0.1 reshape.216
  254.3 0.7 reshape.233
  255.0 2.8 all-to-all-done.2
  257.8 3.2 %all-to-all-start.1 = ((f32[2,1,512]{2,1,0:T(1,128)}), f32[2,1,512]{2,1,0:T(1,128)S(1)}, u32[]{:S(2)}, u32[]{:S(2)}) async-start(f32[2,1,512]{2,1,0:T(1,128)} %reshape.233), calls=%async_computation.1 | async-start | bytes 8192 | tf_op jit(solution)/shard_map/all_to_all | solution.py:121
  261.0 3.3 %fusion.7 = f32[8,2,64,128]{3,2,1,0:T(8,128)S(1)} fusion(f32[8,2,256,2,128]{4,2,3,0,1:T(8,128)} %all-reduce.2.cloned.1.call-done, f32[8,2,64,256]{3,2,1,0:T(8,128)S(1)} %get-tuple-element.19, f32[8,2,64]{2,1,0:T(2,128)S(1)} %broadcast_maximum_fusion.1), kind=kOutput, calls=%fused_computation.11 | convolution fusion | flops 402915328 | bytes 3674112 | tf_op jit(solution)/shard_map/bkrn,bnkd->bkrd/dot_general | solution.py:21
  264.3 0.8 copy.142
  265.2 0.6 broadcast.71
  265.8 0.7 reduce.6
  266.5 0.1 reshape.236
  266.6 0.0 all-to-all-done.1
  266.6 3.5 %all-to-all-start = ((f32[2,8,1,4,16,128]{5,4,3,1,2,0:T(8,128)}), f32[2,8,1,4,16,128]{5,4,3,1,2,0:T(8,128)S(1)}, u32[]{:S(2)}, u32[]{:S(2)}) async-start(f32[2,8,1,4,16,128]{5,4,3,1,2,0:T(8,128)} %bitcast.137), calls=%async_computation | async-start | bytes 1048576 | tf_op jit(solution)/shard_map/all_to_all | solution.py:123
  270.1 0.7 reduce.5
  270.8 0.1 reshape.234
  270.9 0.1 reshape.218
  271.0 0.1 fusion.23
  271.1 0.1 reshape.225
  271.3 5.9 %all-to-all-done = f32[2,8,1,4,16,128]{5,4,3,1,2,0:T(8,128)S(1)} async-done(((f32[2,8,1,4,16,128]{5,4,3,1,2,0:T(8,128)}), f32[2,8,1,4,16,128]{5,4,3,1,2,0:T(8,128)S(1)}, u32[]{:S(2)}, u32[]{:S(2)}) %all-to-all-start) | async-done | bytes 524320 | tf_op jit(solution)/shard_map/all_to_all | solution.py:123
  277.1 0.2 multiply_reduce_fusion
  277.3 0.7 fusion.16
  278.0 0.7 copy.143
  (19 shorter events, 0.2 us)
Async XLA Ops:
  7.2 78.8 %copy-start = (f32[2,128,16,128]{3,2,1,0:T(8,128)S(1)}, f32[2,128,16,128]{3,2,1,0:T(8,128)}, u32[]{:S(2)}) copy-start(f32[2,128,16,128]{3,2,1,0:T(8,128)} %param.7) | copy-start | bytes 6291460
  7.2 40.2 %all-gather.6.cloned.1.call-start = ((), (), s32[]{:S(2)}) async-start(), calls=%async_computation.4 | async-start | bytes 5242880 | tf_op jit(solution)/shard_map/all_gather | solution.py:94
  9.7 76.3 %all-gather.4.cloned.1.call-start = ((), (), s32[]{:S(2)}) async-start(), calls=%async_computation.3 | async-start | bytes 3145728 | tf_op jit(solution)/shard_map/all_gather | solution.py:84
  10.4 234.8 %all-reduce.2.cloned.1.call-start = ((), (), s32[]{:S(2)}) async-start(), calls=%async_computation.5 | async-start | bytes 8388608 | tf_op jit(solution)/shard_map/psum | solution.py:13
  52.0 0.7 copy-start.5
  52.0 5.1 %copy-start.4 = (s32[8]{0:T(128)S(1)}, s32[8]{0:T(128)}, u32[]{:S(2)}) copy-start(s32[8]{0:T(128)} %param.10) | copy-start | bytes 100
  52.0 5.5 %copy-start.1 = (f32[8,1,4,16,128]{4,3,2,1,0:T(8,128)S(1)}, f32[8,1,4,16,128]{4,3,2,1,0:T(8,128)}, u32[]{:S(2)}) copy-start(f32[8,1,4,16,128]{4,3,2,1,0:T(8,128)} %param.8) | copy-start | bytes 786436
  52.0 19.0 %copy-start.3 = (f32[8,1,4,2,2,128]{5,4,3,2,1,0:T(2,128)S(1)}, f32[8,1,4,2,2,128]{5,4,3,2,1,0:T(2,128)}, u32[]{:S(2)}) copy-start(f32[8,1,4,2,2,128]{5,4,3,2,1,0:T(2,128)} %param.9) | copy-start | bytes 196612
  95.6 2.2 copy-start.2
  250.8 7.0 %all-to-all-start.2 = ((f32[2,1,512]{2,1,0:T(1,128)}), f32[2,1,512]{2,1,0:T(1,128)S(1)}, u32[]{:S(2)}, u32[]{:S(2)}) async-start(f32[2,1,512]{2,1,0:T(1,128)} %reshape.235), calls=%async_computation.2 | async-start | bytes 8192 | tf_op jit(solution)/shard_map/all_to_all | solution.py:122
  257.8 8.8 %all-to-all-start.1 = ((f32[2,1,512]{2,1,0:T(1,128)}), f32[2,1,512]{2,1,0:T(1,128)S(1)}, u32[]{:S(2)}, u32[]{:S(2)}) async-start(f32[2,1,512]{2,1,0:T(1,128)} %reshape.233), calls=%async_computation.1 | async-start | bytes 8192 | tf_op jit(solution)/shard_map/all_to_all | solution.py:121
  266.6 10.6 %all-to-all-start = ((f32[2,8,1,4,16,128]{5,4,3,1,2,0:T(8,128)}), f32[2,8,1,4,16,128]{5,4,3,1,2,0:T(8,128)S(1)}, u32[]{:S(2)}, u32[]{:S(2)}) async-start(f32[2,8,1,4,16,128]{5,4,3,1,2,0:T(8,128)} %bitcast.137), calls=%async_computation | async-start | bytes 1048576 | tf_op jit(solution)/shard_map/all_to_all | solution.py:123
Sparse Core Ops, SparseCore 0:
  10.2 37.1 all-gather.5
  49.5 36.4 all-gather.3
  88.4 156.8 all-reduce.1
where the time goes:
time: 286 us; the launch traced here: 285 us
  waiting for transfers between devices  187 us (65%)
  matrix products  36.7 us (13%)
  blocking collectives  16.8 us (6%)
  between operations  14 us (5%)
  local copies, waits for them, and re-layouts  10.3 us (4%)
  starting transfers between devices  10 us (3%)
  other arithmetic  10 us (3%)
    psum x1, waiting for transfers between devices, broadcast(): return lax.psum(kept, axis)  130 us
    all_gather x1, waiting for transfers between devices, on_device(): all_requests = lax.all_gather(kv_cache, 'head', axis=0, tiled=True)  36.9 us
    dot_general x2, matrix products, online_fold(): new_acc = jnp.einsum(pattern, weights, value_rows, precision=HIGH_PRECISION)  18.8 us
    dot_general x2, matrix products, block_fold(): jnp.einsum('bkrd,bnkd->bkrn', query_rows, key_block[:, 0], precision=HIGH...  13.7 us
    all_gather x1, blocking collectives, on_device(): lax.all_gather(decode_q, 'ctx', axis=1, tiled=True)  12.6 us
    all_gather x1, waiting for transfers between devices, on_device(): lax.all_gather(kv_cache, 'ctx', axis=2, tiled=True)  10.6 us
    all_to_all x1, waiting for transfers between devices, on_device(): lax.all_to_all(shaped[2], 'ctx', split_axis=0, concat_axis=0, tiled=True)  5.85 us
  transfers between devices with their start and end apart: 6, of which 5 were waited for; matrix products, arithmetic and copies ran while one was open for 16% of the time, Pallas kernels for 0%

commit v1 on v0

--- a/solution.py
+++ b/solution.py
@@ -6,6 +6,12 @@
 
 NEG_FILL = -1e30
 HIGH_PRECISION = lax.Precision.HIGHEST
+
+
+def in_order(blocks, dim):
+    shape = list(blocks.shape[1:])
+    shape[dim] *= blocks.shape[0]
+    return jnp.moveaxis(blocks, 0, dim).reshape(shape)
 
 
 def broadcast(value, axis, source):
@@ -91,7 +97,19 @@
     prefill_out = jnp.transpose(
         prefill_vals.reshape(req_group, rep_kv, span_rows, group_size, head_dim), (0, 2, 1, 3, 4)
     ).reshape(prefill_q.shape)
-    all_requests = lax.all_gather(kv_cache, "head", axis=0, tiled=True)
+    size = lax.axis_size("head")
+    pairs = [(i, (i + 1) % size) for i in range(size)]
+    back = [(b, a) for a, b in pairs]
+    lower, upper = ([], [])
+    for step in range(size - 1):
+        if step % 2 == 0:
+            lower.append(lax.ppermute(lower[-1] if lower else kv_cache, "head", pairs))
+        else:
+            upper.append(lax.ppermute(upper[-1] if upper else kv_cache, "head", back))
+    pieces = jnp.stack([*lower[::-1], kv_cache, *upper])
+    shift = lax.axis_index("head") - len(lower)
+    pieces = pieces[(jnp.arange(size) - shift) % size]
+    all_requests = in_order(pieces, 0)
     head_cache = broadcast(all_requests, "rep", head_index)
     requests, row_count, step_count, local_heads, unused_dim = decode_q.shape
     kv_heads = local_heads // group_size

time: 286 us -> 272 us (0.951); the launches traced: 285 us -> 266 us
  waiting for transfers between devices: 187 us -> 148 us
  local copies, waits for them, and re-layouts: 10.3 us -> 22 us
  starting transfers between devices: 10 us -> 15.2 us
  other arithmetic: 10 us -> 14.7 us
  blocking collectives: 16.8 us -> 13 us
    all_gather x1 -> x0, waiting for transfers between devices: 36.9 us -> none  [on_device(): all_requests = lax.all_gather(kv_cache, 'head', axis=0, tiled=True)]
    ppermute x0 -> x3, waiting for transfers between devices: none -> 30.5 us  [the longest x2 30.5 us: on_device(): lower.append(lax.ppermute(lower[-1] if lower else kv_cache, 'head', pairs))]
    psum x1, waiting for transfers between devices: 130 us -> 109 us  [broadcast(): return lax.psum(kept, axis)]
    all_gather x1, waiting for transfers between devices: 10.6 us -> 0.02 us  [on_device(): lax.all_gather(kv_cache, 'ctx', axis=2, tiled=True)]
    gather x0 -> x1, local copies, waits for them, and re-layouts: none -> 8.38 us  [on_device(): pieces = pieces[(jnp.arange(size) - shift) % size]]
    another operation x0 -> x1, other arithmetic: none -> 5.27 us  [on_device(): pieces = jnp.stack([*lower[::-1], kv_cache, *upper])]
    ppermute x0 -> x3, starting transfers between devices: none -> 5.14 us  [the longest x2 3.12 us: on_device(): lower.append(lax.ppermute(lower[-1] if lower else kv_cache, 'head', pairs))]
    all_gather x1, blocking collectives: 12.6 us -> 7.76 us  [on_device(): lax.all_gather(decode_q, 'ctx', axis=1, tiled=True)]
  transfers between devices with their start and end apart: 6 -> 8, of which waited for: 5 -> 5; matrix products, arithmetic and copies ran while one was open for 16% -> 25% of each run, Pallas kernels for 0% -> 0%
where the time goes in v1:
time: 272 us; the launch traced here: 266 us
  waiting for transfers between devices  148 us (54%)
  matrix products  37.3 us (14%)
  local copies, waits for them, and re-layouts  22 us (8%)
  between operations  16 us (6%)
  starting transfers between devices  15.2 us (6%)
  other arithmetic  14.7 us (5%)
  blocking collectives  13 us (5%)
    psum x1, waiting for transfers between devices, broadcast(): return lax.psum(kept, axis)  109 us
    ppermute x2, waiting for transfers between devices, on_device(): lower.append(lax.ppermute(lower[-1] if lower else kv_cache, 'head', pairs))  30.5 us
    dot_general x2, matrix products, online_fold(): new_acc = jnp.einsum(pattern, weights, value_rows, precision=HIGH_PRECISION)  19.4 us
    dot_general x2, matrix products, block_fold(): jnp.einsum('bkrd,bnkd->bkrn', query_rows, key_block[:, 0], precision=HIGH...  13.7 us
    gather x1, local copies, waits for them, and re-layouts, on_device(): pieces = pieces[(jnp.arange(size) - shift) % size]  8.38 us
    all_gather x1, blocking collectives, on_device(): lax.all_gather(decode_q, 'ctx', axis=1, tiled=True)  7.76 us
    all_to_all x1, waiting for transfers between devices, on_device(): lax.all_to_all(shaped[2], 'ctx', split_axis=0, concat_axis=0, tiled=True)  5.84 us
  transfers between devices with their start and end apart: 8, of which 5 were waited for; matrix products, arithmetic and copies ran while one was open for 25% of the time, Pallas kernels for 0%

profile of v1, /device:TPU:0, one launch (start us, length us, event | category | flops | bytes accessed | tf_op | source)
XLA Modules:
  0.0 266.4 jit_solution(17719665800390421692)
XLA Ops:
  8.0 0.0 copy-start
  8.0 0.0 all-gather.3.cloned.1.call-start
  8.1 0.5 collective-permute-start
  8.6 2.0 collective-permute-start.2
  10.6 21.2 %collective-permute-done = f32[2,2,256,2,128]{4,3,2,1,0:T(2,128)S(1)} collective-permute-done((f32[2,2,256,2,128]{4,3,2,1,0:T(2,128)}, f32[2,2,256,2,128]{4,3,2,1,0:T(2,128)S(1)}, u32[]{:S(2)}, u32[]{:S(2)}) %collective-permute-start) | collective-permute-done | bytes 1048608 | tf_op jit(solution)/shard_map/ppermute | solution.py:106
  31.8 2.6 collective-permute-start.1
  34.4 2.3 copy.82
  36.7 0.0 all-gather.3.cloned.1.call-update
  36.7 0.0 all-reduce.2.cloned.1.call-start
  36.8 0.0 collective-permute-done.2
  36.8 9.3 %collective-permute-done.1 = f32[2,2,256,2,128]{4,3,2,1,0:T(2,128)} collective-permute-done((f32[2,2,256,2,128]{4,3,2,1,0:T(2,128)S(1)}, f32[2,2,256,2,128]{4,3,2,1,0:T(2,128)}, u32[]{:S(2)}, u32[]{:S(2)}) %collective-permute-start.1) | collective-permute-done | bytes 1048608 | tf_op jit(solution)/shard_map/ppermute | solution.py:106
  46.1 5.3 %pad_maximum_fusion = f32[4,2,2,256,2,128]{5,4,3,2,1,0:T(2,128)} fusion(f32[1,2,2,256,2,128]{5,4,3,2,1,0:T(2,128)} %bitcast.14, f32[1,2,2,256,2,128]{5,4,3,2,1,0:T(2,128)} %bitcast.147, f32[1,2,2,256,2,128]{5,4,3,2,1,0:T(2,128)S(1)} %bitcast.152, f32[1,2,2,256,2,128]{5,4,3,2,1,0:T(2,128)} %bitcast.11), kind=kLoop, calls=%fused_computation.6 | loop fusion | flops 3145728 | bytes 8388608 | tf_op jit(solution)/shard_map/stack | solution.py:109
  51.4 8.4 %gather_fusion = f32[4,2,2,256,2,128]{5,4,3,2,1,0:T(2,128)} fusion(f32[4,2,2,256,2,128]{5,4,3,2,1,0:T(2,128)} %pad_maximum_fusion, s32[1024]{0:T(1024)S(1)} %pad_clamp_fusion), kind=kCustom, calls=%fused_computation | custom fusion | bytes 8388624 | tf_op jit(solution)/shard_map/gather | solution.py:111
  59.8 4.1 %broadcast_select_fusion = f32[4,2,2,256,2,128]{5,4,3,2,1,0:T(2,128)S(1)} fusion(f32[4,2,2,256,2,128]{5,4,3,2,1,0:T(2,128)} %gather_fusion, pred[]{:T(512)S(6)} %eq.5), kind=kLoop, calls=%fused_computation.11 | loop fusion | flops 1048576 | bytes 8388609 | tf_op jit(solution)/shard_map/jit(_where)/select_n | solution.py:18
  63.8 2.5 copy.86
  66.4 0.0 all-reduce.2.cloned.1.call-update
  66.4 0.6 copy-done.5
  67.0 5.2 %all-gather = s32[2,1,8]{2,1,0:T(1,128)S(1)} all-gather(s32[1,1,8]{2,1,0:T(1,128)S(1)} %bitcast.157), channel_id=1, replica_groups=mesh['ctx'=2,'head'=4,'rep'=4] {'ctx'}, dimensions={0}, use_global_device_ids=true | all-gather | bytes 96 | tf_op jit(solution)/shard_map/all_gather | solution.py:118
  72.2 0.1 add_add_fusion
  72.3 0.1 iota_add_fusion.1
  72.4 0.1 broadcast_in_dim.48
  72.5 0.1 le.37
  72.6 7.8 %all_gather.11 = f32[8,2,4,16,128]{4,3,2,1,0:T(8,128)S(1)} all-gather(f32[8,1,4,16,128]{4,3,2,1,0:T(8,128)S(1)} %copy-done.1), channel_id=1, replica_groups=mesh['ctx'=2,'head'=4,'rep'=4] {'ctx'}, dimensions={1}, use_global_device_ids=true | all-gather | bytes 786432 | tf_op jit(solution)/shard_map/all_gather | solution.py:117
  80.4 0.9 copy.87
  81.3 0.1 copy.85
  81.3 0.1 broadcast_in_dim.77
  81.4 0.1 lt.40
  81.6 0.1 broadcast_compare_fusion
  81.7 3.6 %fusion.33 = (f32[8,4,2,8]{3,1,2,0:T(4,128)S(1)}, f32[8,1,4,2,8,4]{4,5,2,3,0,1:T(4,128)S(1)}) fusion(f32[8,1,4,1,2,128]{5,4,3,2,1,0:T(2,128)S(1)} %get-tuple-element.13, pred[4,4]{1,0:T(4,128)(4,1)S(1)} %iota_compare_fusion.1, f32[8,1,4,16,128]{4,3,2,1,0:T(8,128)S(1)} %copy-done.1), kind=kOutput, calls=%fused_computation.72 | convolution fusion | flops 3151360 | bytes 305168 | tf_op jit(solution)/shard_map/artkgd,arskd->artkgs/dot_general | solution.py:149
  85.3 0.6 iota_compare_fusion
  86.0 0.0 all-gather.3.cloned.1.call-done
  86.0 9.6 %fusion = (f32[2,2,1024]{2,1,0:T(2,128)S(1)}, f32[2,2,1024,512]{2,3,1,0:T(8,128)S(1)}) fusion(pred[2,1024,512]{1,2,0:T(8,128)(4,1)S(1)} %iota_compare_fusion, f32[2,2,512,2,128]{4,2,3,0,1:T(8,128)} %all-gather.3.cloned.1.call-done, f32[2,128,16,128]{3,2,1,0:T(8,128)S(1)} %copy-done), kind=kOutput, calls=%fused_computation.3 | convolution fusion | flops 3227512832 | bytes 12599296 | tf_op jit(solution)/shard_map/bkrd,bnkd->bkrn/dot_general | solution.py:42
  95.6 2.2 fusion.1
  97.8 15.4 %divide_bitcast_fusion = f32[2,128,2,8,128]{4,3,1,2,0:T(8,128)S(1)} fusion(f32[2,2,1024]{2,1,0:T(2,128)S(1)} %fusion.1, f32[2,2,512,2,128]{4,2,3,0,1:T(8,128)S(1)} %copy-done.2, f32[2,2,1024,512]{2,3,1,0:T(8,128)S(1)} %get-tuple-element.17, f32[2,2,1024]{2,1,0:T(2,128)S(1)} %broadcast_maximum_fusion, pred[2,1024,512]{1,2,0:T(8,128)(4,1)S(1)} %iota_compare_fusion), kind=kOutput, calls=%fused_computation.21 | convolution fusion | flops 3228041216 | bytes 12615680 | tf_op jit(solution)/shard_map/bkrn,bnkd->bkrd/dot_general | solution.py:27
  113.3 1.5 copy.141
  114.7 109.3 %all-reduce.2.cloned.1.call-done = f32[8,2,256,2,128]{4,2,3,0,1:T(8,128)} async-done(((f32[8,2,256,2,128]{4,2,3,0,1:T(8,128)}), f32[8,2,256,2,128]{4,2,3,0,1:T(8,128)}) %all-reduce.2.cloned.1.call-update) | async-done | bytes 4194320 | tf_op jit(solution)/shard_map/psum | solution.py:19
  224.1 4.1 %fusion.32 = (f32[8,2,64]{2,1,0:T(2,128)S(1)}, f32[8,2,64,256]{3,2,1,0:T(8,128)S(1)}) fusion(f32[8,2,64,128]{3,2,1,0:T(8,128)} %bitcast.151, f32[8,2,256,2,128]{4,2,3,0,1:T(8,128)} %all-reduce.2.cloned.1.call-done, pred[8,64,256]{2,1,0:T(8,128)(4,1)S(1)} %broadcast_compare_fusion), kind=kOutput, calls=%fused_computation.71 | convolution fusion | flops 403438592 | bytes 3805184 | tf_op jit(solution)/shard_map/bkrd,bnkd->bkrn/dot_general | solution.py:42
  228.3 0.1 max_broadcast_in_dim.26
  228.4 0.1 copy.91
  228.4 0.1 reshape.269
  228.5 0.7 reshape.294
  229.2 3.2 %all-to-all-start.1 = ((f32[2,1,512]{2,1,0:T(1,128)}), f32[2,1,512]{2,1,0:T(1,128)S(1)}, u32[]{:S(2)}, u32[]{:S(2)}) async-start(f32[2,1,512]{2,1,0:T(1,128)} %reshape.294), calls=%async_computation.1 | async-start | bytes 8192 | tf_op jit(solution)/shard_map/all_to_all | solution.py:139
  232.4 0.4 fusion.19
  232.9 0.1 reshape.276
  233.0 0.1 copy.101
  233.0 0.1 reshape.277
  233.1 4.0 %fusion.7 = f32[8,2,64,128]{3,2,1,0:T(8,128)} fusion(f32[8,2,256,2,128]{4,2,3,0,1:T(8,128)} %all-reduce.2.cloned.1.call-done, f32[8,2,64,256]{3,2,1,0:T(8,128)S(1)} %get-tuple-element.19, f32[8,2,64]{2,1,0:T(2,128)S(1)} %broadcast_maximum_fusion.1), kind=kOutput, calls=%fused_computation.14 | convolution fusion | flops 402915328 | bytes 3674112 | tf_op jit(solution)/shard_map/bkrn,bnkd->bkrd/dot_general | solution.py:27
  237.1 0.7 reshape.296
  237.8 1.9 copy.142
  239.7 3.3 %all-to-all-start.2 = ((f32[2,1,512]{2,1,0:T(1,128)}), f32[2,1,512]{2,1,0:T(1,128)S(1)}, u32[]{:S(2)}, u32[]{:S(2)}) async-start(f32[2,1,512]{2,1,0:T(1,128)} %reshape.296), calls=%async_computation.2 | async-start | bytes 8192 | tf_op jit(solution)/shard_map/all_to_all | solution.py:140
  242.9 0.5 broadcast.144
  243.4 0.7 reduce.5
  244.1 0.1 reshape.295
  244.2 0.1 reshape.271
  244.3 2.4 all-to-all-done.2
  246.7 3.5 %all-to-all-start = ((f32[2,8,1,4,16,128]{5,4,3,1,2,0:T(8,128)}), f32[2,8,1,4,16,128]{5,4,3,1,2,0:T(8,128)S(1)}, u32[]{:S(2)}, u32[]{:S(2)}) async-start(f32[2,8,1,4,16,128]{5,4,3,1,2,0:T(8,128)} %bitcast.144), calls=%async_computation | async-start | bytes 1048576 | tf_op jit(solution)/shard_map/all_to_all | solution.py:141
  250.2 0.7 reduce.6
  250.9 0.1 reshape.297
  251.0 0.1 fusion.23
  251.2 0.1 reshape.278
  251.3 5.8 %all-to-all-done = f32[2,8,1,4,16,128]{5,4,3,1,2,0:T(8,128)S(1)} async-done(((f32[2,8,1,4,16,128]{5,4,3,1,2,0:T(8,128)}), f32[2,8,1,4,16,128]{5,4,3,1,2,0:T(8,128)S(1)}, u32[]{:S(2)}, u32[]{:S(2)}) %all-to-all-start) | async-done | bytes 524320 | tf_op jit(solution)/shard_map/all_to_all | solution.py:141
  257.1 0.2 multiply_reduce_fusion
  257.4 0.7 fusion.16
  258.0 0.7 copy.143
  (27 shorter events, 0.2 us)
Async XLA Ops:
  8.0 78.0 %copy-start = (f32[2,128,16,128]{3,2,1,0:T(8,128)S(1)}, f32[2,128,16,128]{3,2,1,0:T(8,128)}, u32[]{:S(2)}) copy-start(f32[2,128,16,128]{3,2,1,0:T(8,128)} %param.7) | copy-start | bytes 6291460
  8.0 78.0 %all-gather.3.cloned.1.call-start = ((), (), s32[]{:S(2)}) async-start(), calls=%async_computation.3 | async-start | bytes 3145728 | tf_op jit(solution)/shard_map/all_gather | solution.py:90
  8.1 23.7 %collective-permute-start = (f32[2,2,256,2,128]{4,3,2,1,0:T(2,128)}, f32[2,2,256,2,128]{4,3,2,1,0:T(2,128)S(1)}, u32[]{:S(2)}, u32[]{:S(2)}) collective-permute-start(f32[2,2,256,2,128]{4,3,2,1,0:T(2,128)} %param.6), channel_id=1, source_target_pairs={{0,4},{4,8},{8,12},{12,0},{1,5},{5,9},{9,13},{13,1},{2,6},{6,10},{... | collective-permute-start | bytes 3145736 | tf_op jit(solution)/shard_map/ppermute | solution.py:106
  8.6 28.2 %collective-permute-start.2 = (f32[2,2,256,2,128]{4,3,2,1,0:T(2,128)}, f32[2,2,256,2,128]{4,3,2,1,0:T(2,128)}, u32[]{:S(2)}, u32[]{:S(2)}) collective-permute-start(f32[2,2,256,2,128]{4,3,2,1,0:T(2,128)} %param.6), channel_id=1, source_target_pairs={{4,0},{8,4},{12,8},{0,12},{5,1},{9,5},{13,9},{1,13},{6,2},{10,6},{... | collective-permute-start | bytes 3145736 | tf_op jit(solution)/shard_map/ppermute | solution.py:108
  31.8 14.3 %collective-permute-start.1 = (f32[2,2,256,2,128]{4,3,2,1,0:T(2,128)S(1)}, f32[2,2,256,2,128]{4,3,2,1,0:T(2,128)}, u32[]{:S(2)}, u32[]{:S(2)}) collective-permute-start(f32[2,2,256,2,128]{4,3,2,1,0:T(2,128)S(1)} %collective-permute-done), channel_id=1, source_target_pairs={{0,4},{4,8},{8,12},{12,0},{1,5},{5,9},{9,13},{13,1},{2,6},{6,10},{... | collective-permute-start | bytes 3145736 | tf_op jit(solution)/shard_map/ppermute | solution.py:106
  36.7 187.4 %all-reduce.2.cloned.1.call-start = ((), (), s32[]{:S(2)}) async-start(), calls=%async_computation.4 | async-start | bytes 8388608 | tf_op jit(solution)/shard_map/psum | solution.py:19
  66.4 0.7 copy-start.5
  66.4 5.9 %copy-start.4 = (s32[8]{0:T(128)S(1)}, s32[8]{0:T(128)}, u32[]{:S(2)}) copy-start(s32[8]{0:T(128)} %param.10) | copy-start | bytes 100
  66.4 6.2 %copy-start.1 = (f32[8,1,4,16,128]{4,3,2,1,0:T(8,128)S(1)}, f32[8,1,4,16,128]{4,3,2,1,0:T(8,128)}, u32[]{:S(2)}) copy-start(f32[8,1,4,16,128]{4,3,2,1,0:T(8,128)} %param.8) | copy-start | bytes 786436
  66.4 15.2 %copy-start.3 = (f32[8,1,4,2,2,128]{5,4,3,2,1,0:T(2,128)S(1)}, f32[8,1,4,2,2,128]{5,4,3,2,1,0:T(2,128)}, u32[]{:S(2)}) copy-start(f32[8,1,4,2,2,128]{5,4,3,2,1,0:T(2,128)} %param.9) | copy-start | bytes 196612
  95.6 2.2 copy-start.2
  229.2 10.4 %all-to-all-start.1 = ((f32[2,1,512]{2,1,0:T(1,128)}), f32[2,1,512]{2,1,0:T(1,128)S(1)}, u32[]{:S(2)}, u32[]{:S(2)}) async-start(f32[2,1,512]{2,1,0:T(1,128)} %reshape.294), calls=%async_computation.1 | async-start | bytes 8192 | tf_op jit(solution)/shard_map/all_to_all | solution.py:139
  239.7 7.1 %all-to-all-start.2 = ((f32[2,1,512]{2,1,0:T(1,128)}), f32[2,1,512]{2,1,0:T(1,128)S(1)}, u32[]{:S(2)}, u32[]{:S(2)}) async-start(f32[2,1,512]{2,1,0:T(1,128)} %reshape.296), calls=%async_computation.2 | async-start | bytes 8192 | tf_op jit(solution)/shard_map/all_to_all | solution.py:140
  246.7 10.4 %all-to-all-start = ((f32[2,8,1,4,16,128]{5,4,3,1,2,0:T(8,128)}), f32[2,8,1,4,16,128]{5,4,3,1,2,0:T(8,128)S(1)}, u32[]{:S(2)}, u32[]{:S(2)}) async-start(f32[2,8,1,4,16,128]{5,4,3,1,2,0:T(8,128)} %bitcast.144), calls=%async_computation | async-start | bytes 1048576 | tf_op jit(solution)/shard_map/all_to_all | solution.py:141
Sparse Core Ops, SparseCore 0:
  36.8 34.7 all-gather.2
Sparse Core Ops, SparseCore 1:
  66.5 157.6 all-reduce.1
